TPU v7x, 256 devices: a whole 4x4x8 slice. The times are simulated.
256 devices in a mesh: leaf: 64 (over z, y, core), blk: 4 (over x).
Axes of the slice: x: 4, y: 4, z: 8, core: 2. Of those that a mesh axis runs over, the one named last changes fastest.
Arguments:
- parent_inverse: bfloat16 [64, 512, 512], P('leaf', None, 'blk'), as said below
- leaf_inverse: bfloat16 [896, 512, 512], P('leaf', 'blk'), as said below
- coupling: bfloat16 [896, 512, 512], P('leaf', 'blk'), may hold values from -0.25 to 0.25
- sensitivity: bfloat16 [896, 512, 512], P('leaf', 'blk'), may hold values from -0.25 to 0.25
- parent_of: int32 [896, 1], P('leaf'), may hold values from 0 to 63
- leaf_field: bfloat16 [896, 512], P('leaf'), may hold values from -6 to 6
- parent_field: bfloat16 [64, 512], P('leaf', 'blk'), may hold values from -6 to 6
Outputs:
- leaf_grad: float32 [896, 512], P('leaf', 'blk')
- coupling_grad: float32 [64, 512], P('leaf', 'blk')
Inputs may be any that keep to these rules, and one draw needn't show every extreme that they name: `parent_of`: every one of the 64 separator supernodes is the parent of at least one leaf. `parent_inverse`: lower triangular with a positive diagonal. `leaf_inverse`: lower triangular with a positive diagonal.
All inputs are finite; a program needn't handle non-finite values.
Results may differ from a plain program's by a relative error of at most 0.0006.
Values may be sent and summed in bfloat16 or wider, within the bound.
A program may use at most 128 MiB of HBM per device.

v0:
```python
import jax
import jax.numpy as jnp
from jax import lax
from jax.sharding import PartitionSpec as P


def body(parent_inverse, leaf_inverse, coupling, sensitivity, parent_of, leaf_field, parent_field):
    count = coupling.shape[0]
    share = coupling.shape[1]
    width = coupling.shape[2]
    offset = lax.axis_index("blk") * share
    cov_rows = jnp.einsum(
        "pkr,pkc->prc",
        parent_inverse,
        lax.all_gather(parent_inverse, "blk", axis=2, tiled=True),
        preferred_element_type=jnp.float32,
    ).astype(jnp.bfloat16)
    parent_ids = parent_of[:, 0]
    initial = (
        jnp.zeros((count, share, width), jnp.bfloat16),
        jnp.zeros((count, share), jnp.bfloat16),
    )
    pieces = (
        lax.all_gather(cov_rows, "leaf", axis=0, tiled=True),
        lax.all_gather(parent_field, "leaf", axis=0, tiled=True),
    )
    number = pieces[0].shape[0]
    inside = (parent_ids >= 0) & (parent_ids < number)
    position = jnp.clip(parent_ids, 0, number - 1)
    taken_cov = jnp.take(pieces[0], position, axis=0)
    taken_field = jnp.take(pieces[1], position, axis=0)
    chosen_cov = jnp.where(inside[:, None, None], taken_cov, initial[0])
    chosen_field = jnp.where(inside[:, None], taken_field, initial[1])
    panel = coupling
    mixed = jnp.einsum(
        "lik,lkc->lic",
        panel,
        lax.all_gather(leaf_inverse, "blk", axis=1, tiled=True),
        preferred_element_type=jnp.float32,
    ).astype(jnp.bfloat16)
    cross = jnp.zeros((count, share, width), jnp.float32) - jnp.einsum(
        "lrk,lkc->lrc",
        chosen_cov,
        lax.all_gather(mixed, "blk", axis=1, tiled=True),
        preferred_element_type=jnp.float32,
    )
    cross_half = cross.astype(jnp.bfloat16)
    panel = coupling
    update = lax.psum_scatter(
        jnp.einsum("lik,lia->kla", panel, cross_half, preferred_element_type=jnp.float32),
        "blk",
        scatter_dimension=0,
        tiled=True,
    )
    factor = leaf_inverse.astype(jnp.float32)
    partial_diag = jnp.sum(factor * factor, 1) - jnp.einsum(
        "lka,kla->la", factor, update, precision=lax.Precision.HIGHEST
    )
    diagonal = lax.psum_scatter(partial_diag, "blk", scatter_dimension=1, tiled=True)
    value = lax.dynamic_slice_in_dim(leaf_field, offset, share, 1).astype(jnp.float32)
    leaf_grad = 0.5 * (diagonal - value * value)
    returned = jnp.sum(sensitivity.astype(jnp.float32) * cross, 2) - chosen_field.astype(
        jnp.float32
    ) * jnp.einsum("lab,lb->la", sensitivity, leaf_field, preferred_element_type=jnp.float32)
    parent_total = lax.axis_size("leaf")
    owners = (
        parent_ids[:, None] == lax.broadcasted_iota(jnp.int32, (count, parent_total), 1)
    ).astype(jnp.float32)
    spread = jnp.einsum("lp,la->pa", owners, returned, precision=lax.Precision.HIGHEST)
    coupling_grad = lax.psum_scatter(spread, "leaf", scatter_dimension=0, tiled=True)
    return (leaf_grad, coupling_grad)


def solution(mesh):
    in_specs = (
        P("leaf", None, "blk"),
        P("leaf", "blk", None),
        P("leaf", "blk", None),
        P("leaf", "blk", None),
        P("leaf", None),
        P("leaf", None),
        P("leaf", "blk"),
    )
    out_specs = (P("leaf", "blk"), P("leaf", "blk"))
    return jax.shard_map(body, mesh=mesh, in_specs=in_specs, out_specs=out_specs, check_vma=False)
```

profile of v0, /device:TPU:1, one launch (start us, length us, event | category | flops | bytes accessed | tf_op | source)
XLA Modules:
  0.0 594.6 jit_solution(6731102882643299972)
XLA Ops:
  7.2 0.7 all-gather.6.cloned.1.call-update
  8.0 13.5 %all_gather.15 = bf16[1,512,512]{2,1,0:T(8,128)(2,1)S(1)} all-gather(bf16[1,512,128]{2,1,0:T(8,128)(2,1)} %param.7), channel_id=1, replica_groups=mesh['leaf'=64,'blk'=4] {'blk'}, dimensions={2}, use_global_device_ids=true | all-gather | bytes 655360 | tf_op jit(solution)/shard_map/all_gather | solution.py:15
  21.4 1.8 convolution_convert_fusion.1
  23.4 67.2 %all-gather.6.cloned.1.call-done = bf16[14,512,512]{2,1,0:T(8,128)(2,1)} async-done(((bf16[14,128,512]{2,1,0:T(8,128)(2,1)}), bf16[14,512,512]{2,1,0:T(8,128)(2,1)}) %all-gather.6.cloned.1.call-update) | async-done | bytes 7340048 | tf_op jit(solution)/shard_map/all_gather | solution.py:38
  90.6 5.4 convolution_convert_fusion
  96.1 81.6 %all-gather.10.cloned.1.call-done = bf16[8192,512]{1,0:T(8,128)(2,1)} async-done(((bf16[128,512]{1,0:T(8,128)(2,1)}), bf16[8192,512]{1,0:T(8,128)(2,1)}) %all-gather.10.cloned.1.call-update) | async-done | bytes 8388624 | tf_op jit(solution)/shard_map/all_gather | solution.py:24
  177.7 5.3 gather_fusion
  183.0 70.1 %all-gather.8.cloned.1.call-done = bf16[14,512,512]{2,1,0:T(8,128)(2,1)} async-done(((bf16[14,128,512]{2,1,0:T(8,128)(2,1)}), bf16[14,512,512]{2,1,0:T(8,128)(2,1)}) %all-gather.8.cloned.1.call-update) | async-done | bytes 7340048 | tf_op jit(solution)/shard_map/all_gather | solution.py:44
  253.2 5.4 multiply_reduce_fusion.1
  258.6 7.3 %convolution_bitcast_fusion = f32[512,14,512]{0,2,1:T(8,128)} fusion(bf16[14,128,512]{2,1,0:T(8,128)(2,1)S(1)} %copy-done, f32[14,128,512]{2,1,0:T(8,128)S(1)} %get-tuple-element.5), kind=kOutput, calls=%fused_computation.2 | convolution fusion | flops 941359104 | bytes 20185088 | tf_op jit(solution)/shard_map/lik,lia->kla/dot_general | solution.py:50
  266.0 0.6 copy-done.2
  266.6 41.6 %all-gather.1 = bf16[64,1,128]{2,1,0:T(2,128)(2,1)S(1)} all-gather(bf16[1,1,128]{2,1,0:T(2,128)(2,1)S(1)} %bitcast.40), channel_id=1, replica_groups=mesh['leaf'=64,'blk'=4] {'leaf'}, dimensions={0}, use_global_device_ids=true | all-gather | bytes 16640 | tf_op jit(solution)/shard_map/all_gather | solution.py:25
  308.2 0.6 gather_fusion.1
  308.8 0.6 dynamic-slice
  309.4 1.9 multiply_reduce_fusion.2
  311.3 2.1 fusion.10
  313.4 0.3 fusion.13
  313.7 241.7 %all-reduce = f32[64,128]{1,0:T(8,128)S(1)} all-reduce(f32[64,128]{1,0:T(8,128)S(1)} %fusion.13), channel_id=5, replica_groups=mesh['leaf'=64,'blk'=4] {'leaf'}, use_global_device_ids=true, to_apply=%region_4.5.clone | all-reduce | flops 8192 | bytes 65536
  555.4 5.1 copy.17
  560.5 3.2 multiply_reduce_fusion
  563.8 0.6 sub.13
  564.4 1.2 constant_dynamic-slice_fusion
  565.6 21.2 %reduce-scatter.5.cloned.1.call-done = f32[14,128]{1,0:T(8,128)} async-done(((f32[14,512]{1,0:T(8,128)}), f32[14,128]{1,0:T(8,128)}) %reduce-scatter.5.cloned.1.call-update) | async-done | bytes 7184 | tf_op jit(solution)/shard_map/reduce_scatter | solution.py:59
  586.7 1.3 subtract_multiply_fusion
  (24 shorter events, 0.3 us)
Async XLA Ops:
  7.2 83.4 %copy-start = (bf16[14,128,512]{2,1,0:T(8,128)(2,1)S(1)}, bf16[14,128,512]{2,1,0:T(8,128)(2,1)}, u32[]{:S(2)}) copy-start(bf16[14,128,512]{2,1,0:T(8,128)(2,1)} %param.9) | copy-start | bytes 5505028
  7.2 83.4 %all-gather.6.cloned.1.call-start = ((), (), s32[]{:S(2)}) async-start(), calls=%async_computation.2 | async-start | bytes 9175040 | tf_op jit(solution)/shard_map/all_gather | solution.py:38
  7.9 169.8 %all-gather.10.cloned.1.call-start = ((), (), s32[]{:S(2)}) async-start(), calls=%async_computation.6 | async-start | bytes 8519680 | tf_op jit(solution)/shard_map/all_gather | solution.py:24
  23.3 72.8 %copy-start.3 = (s32[14,1]{0,1:T(1,128)S(1)}, s32[14,1]{0,1:T(1,128)}, u32[]{:S(2)}) copy-start(s32[14,1]{0,1:T(1,128)} %param.11) | copy-start | bytes 172
  23.3 229.9 %all-gather.8.cloned.1.call-start = ((), (), s32[]{:S(2)}) async-start(), calls=%async_computation.3 | async-start | bytes 9175040 | tf_op jit(solution)/shard_map/all_gather | solution.py:44
  96.0 459.4 %reduce-scatter.3.cloned.1.call-start = ((), (), s32[]{:S(2)}) async-start(), calls=%async_computation.4 | async-start | bytes 18350080 | tf_op jit(solution)/shard_map/reduce_scatter | solution.py:49
  265.9 0.7 copy-start.2
  265.9 42.9 %copy-start.4 = (u32[256]{0:T(256)S(1)}, u32[256]{0:T(256)}, u32[]{:S(2)}) copy-start(u32[256]{0:T(256)} %constant.58) | copy-start | bytes 3076
  265.9 45.4 %copy-start.1 = (bf16[14,512]{1,0:T(8,128)(2,1)S(1)}, bf16[14,512]{1,0:T(8,128)(2,1)}, u32[]{:S(2)}) copy-start(bf16[14,512]{1,0:T(8,128)(2,1)} %param.12) | copy-start | bytes 43012
  266.0 320.8 %reduce-scatter.5.cloned.1.call-start = ((), (), s32[]{:S(2)}) async-start(), calls=%async_computation.5 | async-start | bytes 40960 | tf_op jit(solution)/shard_map/reduce_scatter | solution.py:59
Sparse Core Ops, SparseCore 0:
  9.8 80.6 all-gather.5
  93.3 84.3 all-gather.9
  179.5 73.6 all-gather.7
  266.1 134.9 reduce-scatter.2
  564.5 22.1 reduce-scatter.4
where the time goes:
time: 596 us; the launch traced here: 595 us
  blocking collectives  297 us (50%)
  waiting for transfers between devices  241 us (40%)
  matrix products  22.4 us (4%)
  between operations  13.9 us (2%)
  local copies, waits for them, and re-layouts  13.4 us (2%)
  other arithmetic  7.09 us (1%)
    unnamed x1, blocking collectives  242 us
    all_gather x1, waiting for transfers between devices, body(): lax.all_gather(cov_rows, 'leaf', axis=0, tiled=True)  81.6 us
    all_gather x1, waiting for transfers between devices, body(): lax.all_gather(mixed, 'blk', axis=1, tiled=True)  70.1 us
    all_gather x1, waiting for transfers between devices, body(): lax.all_gather(leaf_inverse, 'blk', axis=1, tiled=True)  67.2 us
    all_gather x1, blocking collectives, body(): lax.all_gather(parent_field, 'leaf', axis=0, tiled=True)  41.6 us
    reduce_scatter x1, waiting for transfers between devices, body(): lax.psum_scatter(partial_diag, 'blk', scatter_dimension=1, tiled=True)  21.2 us
    all_gather x1, blocking collectives, body(): lax.all_gather(parent_inverse, 'blk', axis=2, tiled=True)  13.5 us
  transfers between devices with their start and end apart: 5, of which 4 were waited for; matrix products, arithmetic and copies ran while one was open for 3% of the time, Pallas kernels for 0%

commit v1 on v0

v1 whole, which is shorter than its diff:
```python
import jax
import jax.numpy as jnp
from jax import lax
from jax.experimental import pallas as pl
from jax.experimental.pallas import tpu as pltpu
from jax.sharding import PartitionSpec as P

MESH = pl.DeviceIdType.MESH
F32 = jnp.float32
BF16 = jnp.bfloat16
B = 128
W = 512
X, Y, Z = 4, 4, 8
GROUPS = 64
MAXN = 4
EVEN = ((0, 0), (1, 0), (2, 0), (3, 0), (2, 2))
ODD = ((1, 1), (2, 1), (3, 1), (3, 3), (3, 2))
YFIRST = 2


def transposed_dot(a, b):
    return lax.dot_general(a, b, (((0,), (0,)), ((), ())), preferred_element_type=F32)


def at_block(i):
    return pl.ds(pl.multiple_of(i * B, B), B)


def kernel(
    pof, pinv, linv, coup, sens, field, pfield,
    lg_out, cg_out,
    cbuf, lbuf, sbuf, ublk, mixed, mixed_half, crossed, factor, cov, ga, gb, picked,
    fld, masks, fin, got_x, acc, got_all,
    send_p, send_c, send_l, send_s, send_u, send_ring, send_cross, send_f, send_g,
    recv_p, recv_cl, recv_s, recv_u, recv_a, recv_b, recv_cross, recv_f, recv_g,
):
    leaf = lax.axis_index("leaf")
    x = lax.axis_index("blk")
    z = leaf // 8
    y = (leaf // 2) % 4
    c = leaf % 2

    def count(xx):
        return 3 + (xx + c + 1) % 2

    def first(xx):
        return 3 * xx + (xx + 1 - c) // 2

    def plane(d):
        return (x + d) % X

    def remote(src, dst, send, recv, to):
        return pltpu.make_async_remote_copy(src, dst, send, recv, device_id=to, device_id_type=MESH)

    mine = count(x)
    base = first(x)
    counts = [count(plane(d)) for d in range(X)]
    firsts = [first(plane(d)) for d in range(X)]

    def arrived(ref, sem):
        pltpu.make_async_copy(ref, ref, sem).wait()

    barrier = pltpu.get_barrier_semaphore()
    for d in range(1, X):
        pl.semaphore_signal(barrier, inc=1, device_id=(leaf, plane(d)), device_id_type=MESH)

    @pl.loop(1, GROUPS)
    def _(d):
        pl.semaphore_signal(barrier, inc=1, device_id=((leaf + d) % GROUPS, x), device_id_type=MESH)

    zero = jnp.zeros((MAXN, B, B), BF16)
    lbuf[:, 0:B, B : 2 * B] = zero
    lbuf[:, 2 * B : 3 * B, 3 * B : 4 * B] = zero
    factor[0:B, B : 2 * B] = zero[0]
    factor[2 * B : 3 * B, 3 * B : 4 * B] = zero[0]
    fin[...] = jnp.zeros_like(fin)
    pl.semaphore_wait(barrier, X - 1 + GROUPS - 1)

    def slot_a(yy, zz, core=c):
        return core * 32 + zz * 4 + yy

    def slot_b(yy, zz, core=c):
        return core * 32 + yy * 8 + zz

    def own_slot(k):
        return ga.at[slot_a(y, z), k] if k < YFIRST else gb.at[slot_b(y, z), k - YFIRST]

    routes = [(0, k, k) for k in range(4)] + [(1, k, k + 1) for k in range(3)] + [(2, 4, 2), (3, 3, 3)]

    for at in range(X):
        @pl.when(x == at)
        def _(at=at):
            for plane_at, k, rb in routes:
                if plane_at == at:
                    block = pinv.at[0, rb * B : (rb + 1) * B]
                    remote(block, own_slot(k), send_p, recv_p, (leaf, plane(2))).start()
                    pltpu.make_async_copy(block, own_slot(k), recv_p).start()
            if at == 2:
                for d in (1, 3):
                    remote(pinv.at[0, 3 * B :], own_slot(4), send_p, recv_p, (leaf, plane(d))).start()

    def c_copy(d, l):
        return remote(coup.at[firsts[d] + l], cbuf.at[l, at_block(x)], send_c, recv_cl.at[l], (leaf, plane(d)))

    def s_copy(d, l):
        return remote(sens.at[firsts[d] + l], sbuf.at[l, at_block(x)], send_s, recv_s.at[l], (leaf, plane(d)))

    def l_copy(d, l, cb):
        return remote(linv.at[firsts[d] + l, :, at_block(cb)], lbuf.at[l, at_block(x), at_block(cb)],
                      send_l, recv_cl.at[l], (leaf, plane(d)))

    def for_leaf(l, d, fn):
        if l < MAXN - 1:
            fn()
        else:
            pl.when(counts[d] == MAXN)(fn)

    def send_s_panels(leaves):
        for l in leaves:
            for d in (1, 3, 2):
                for_leaf(l, d, lambda l=l, d=d: s_copy(d, l).start())

    for l in range(MAXN):
        for d in (1, 3, 2):
            def send(l=l, d=d):
                c_copy(d, l).start()

                @pl.loop(0, x + 1)
                def _(cb):
                    l_copy(d, l, cb).start()

            for_leaf(l, d, send)
    send_s_panels(range(2))

    @pl.loop(0, mine)
    def _(l):
        pltpu.make_async_copy(coup.at[base + l], cbuf.at[l, at_block(x)], recv_cl.at[l]).start()
        pltpu.make_async_copy(sens.at[base + l], sbuf.at[l, at_block(x)], recv_s.at[l]).start()

        @pl.loop(0, x + 1)
        def _(cb):
            pltpu.make_async_copy(
                linv.at[base + l, :, at_block(cb)], lbuf.at[l, at_block(x), at_block(cb)], recv_cl.at[l]).start()

    def up(n, v, by):
        return (v + by) % n

    def hop(which, ref, along_y, way, sem):
        by = 1 - 2 * way
        to = (z * 8 + up(Y, y, by) * 2 + c, x) if along_y else (up(Z, z, by) * 8 + y * 2 + c, x)
        remote(ref, ref, send_ring.at[which], sem, to).start()

    def a_first(step):
        for way in range(2):
            yy = up(Y, y, -(1 - 2 * way) * (step - 1))
            hop(0, ga.at[slot_a(yy, z)] if step == 1 else ga.at[slot_a(yy, z), way], True, way, recv_a.at[step - 1])

    def a_second(group, step):
        for way in range(2):
            zz = up(Z, z, -(1 - 2 * way) * (step - 1))
            sem = recv_a.at[2 + group * 4 + step - 1]
            if group == 1:
                for side in (way,) if step == 4 else range(2):
                    hop(0, ga.at[slot_a(up(Y, y, 2 * side - 1), zz)], False, way, sem)
            else:
                slot = slot_a(up(Y, y, group), zz)
                hop(0, ga.at[slot, way] if step == 4 else ga.at[slot], False, way, sem)

    def b_first(step):
        for way in range(2):
            slot = slot_b(y, up(Z, z, -(1 - 2 * way) * (step - 1)))
            ref = gb.at[slot, :, way * 64 : way * 64 + 64] if step == 4 else gb.at[slot]
            hop(1, ref, False, way, recv_b.at[step - 1])

    def b_second(group, step):
        for way in range(2):
            yy = up(Y, y, -(1 - 2 * way) * (step - 1))
            sem = recv_b.at[4 + group * 2 + step - 1]
            if group in (0, 4):
                slot = slot_b(yy, up(Z, z, group))
                hop(1, gb.at[slot, :, way * 64 : way * 64 + 64] if step == 2 else gb.at[slot], True, way, sem)
            else:
                for side in (way,) if step == 2 else range(2):
                    hop(1, gb.at[slot_b(yy, up(Z, z, (2 * side - 1) * group))], True, way, sem)

    def across_a(zz):
        ref = ga.at[pl.ds(slot_a(0, zz), 4)]
        remote(ref, ref, send_cross.at[0], recv_cross.at[0], (leaf + 1 - 2 * c, x)).start()

    def across_b(yy):
        ref = gb.at[pl.ds(slot_b(yy, 0), 8)]
        remote(ref, ref, send_cross.at[1], recv_cross.at[1], (leaf + 1 - 2 * c, x)).start()

    def a_first_done(step):
        arrived(ga.at[0 : 2 if step == 1 else 1], recv_a.at[step - 1])
        if step == 1:
            a_first(2)
            a_second(1, 1)
        else:
            a_second(2, 1)
            across_a(z)

    def a_second_done(group, step):
        size = (2 if step == 4 else 4) if group == 1 else (1 if step == 4 else 2)
        arrived(ga.at[0:size], recv_a.at[2 + group * 4 + step - 1])
        if step < 4:
            a_second(group, step + 1)

    def b_first_done(step):
        arrived(gb.at[0 : 1 if step == 4 else 2], recv_b.at[step - 1])
        if step < 4:
            b_first(step + 1)
        b_second(step, 1)
        if step == 4:
            across_b(y)

    def b_second_done(group, step):
        size = (1 if step == 2 else 2) if group in (0, 4) else (2 if step == 2 else 4)
        arrived(gb.at[0:size], recv_b.at[4 + group * 2 + step - 1])
        if step == 1:
            b_second(group, 2)

    arrived(picked.at[0, 0], recv_p)
    b_first(1)
    a_first(1)
    b_second(0, 1)
    a_second(0, 1)
    b_first_done(1)
    a_first_done(1)
    b_second_done(0, 1)
    a_second_done(0, 1)
    b_first_done(2)
    a_first_done(2)
    a_second_done(0, 2)
    b_second_done(1, 1)
    a_second_done(1, 1)
    b_first_done(3)
    a_second_done(2, 1)
    a_second_done(0, 3)
    b_second_done(2, 1)
    a_second_done(1, 2)
    b_first_done(4)
    a_second_done(2, 2)
    for way in range(2):
        across_a(up(Z, z, 2 * way - 1))
    b_second_done(3, 1)
    a_second_done(1, 3)
    a_second_done(2, 3)
    for step in range(2, 4):
        for way in range(2):
            across_a(up(Z, z, (2 * way - 1) * step))
    b_second_done(4, 1)
    for way in range(2):
        across_b(up(Y, y, 2 * way - 1))
    for group in range(3):
        a_second_done(group, 4)
    across_a(up(Z, z, 4))
    for group in range(5):
        b_second_done(group, 2)
    across_b(up(Y, y, 2))
    arrived(ga.at[0:32], recv_cross.at[0])
    arrived(gb.at[0:32], recv_cross.at[1])

    odd = x % 2

    def u_copy(i, l, some):
        ref = picked.at[i, l, pl.ds(0, 4)] if some == 0 else picked.at[i, l, pl.ds(4, 1)]
        dst = ublk.at[l, odd, pl.ds(0, 4)] if some == 0 else ublk.at[l, odd, pl.ds(4, 1)]
        return remote(ref, dst, send_u, recv_u.at[l], (leaf, plane(1 + 2 * i)))

    def chosen(j):
        p = pof[0, j]
        half = (p & 1) * 32
        yy = (p >> 1) & 3
        zz = p >> 3
        a = half + zz * 4 + yy
        b = half + yy * 8 + zz
        return [lambda k=k: ga[a, k] for k in range(YFIRST)] + [lambda k=k: gb[b, k] for k in range(5 - YFIRST)]

    for l in range(MAXN):
        for i in range(2):
            def pick(l=l, i=i):
                block = chosen(firsts[1 + 2 * i] + l)

                @pl.when(x < 2)
                def _():
                    for k in range(4):
                        picked[i, l, k] = block[k]()
                    u_copy(i, l, 0).start()

                @pl.when(x >= 2)
                def _():
                    picked[i, l, 4] = block[4]()
                    u_copy(i, l, 1).start()

            for_leaf(l, 1 + 2 * i, pick)
    send_s_panels(range(2, MAXN))

    for l in range(MAXN):
        def keep(l=l):
            block = chosen(base + l)
            for k in range(5):
                ublk[l, odd, k] = block[k]()

        for_leaf(l, 0, keep)

    fld[0:14] = field[...].astype(F32)
    place = lax.broadcasted_iota(jnp.int32, (GROUPS, B), 0)
    for xx in range(X):
        for l in range(MAXN):
            p = pof[0, jnp.minimum(first(xx) + l, 13)]
            if l == MAXN - 1:
                p = jnp.where(count(xx) == MAXN, p, -1)
            masks[xx * MAXN + l] = jnp.where(place == p, 1.0, 0.0)

    for at, blocks in enumerate((4, 3, 3, 1)):
        @pl.when(x == at)
        def _(blocks=blocks):
            arrived(pinv.at[0, 0 : blocks * B], send_p)
    arrived(ga.at[0:31], send_ring.at[0])
    arrived(gb.at[0:31], send_ring.at[1])
    arrived(ga.at[0:32], send_cross.at[0])
    arrived(gb.at[0:32], send_cross.at[1])

    @pl.loop(0, mine)
    def _(l):
        arrived(ga.at[0:13], recv_cl.at[l])

        left = jnp.dot(cbuf[l], lbuf[l, :, 0 : 2 * B], preferred_element_type=F32)
        mixed[l, :, 0 : 2 * B] = left
        mixed_half[l, :, 0 : 2 * B] = left.astype(BF16)
        right = jnp.dot(cbuf[l, :, 2 * B :], lbuf[l, 2 * B :, 2 * B :], preferred_element_type=F32)
        mixed[l, :, 2 * B :] = right
        mixed_half[l, :, 2 * B :] = right.astype(BF16)
        low = lbuf[l, :, 0 : 2 * B].astype(F32)
        high = lbuf[l, 2 * B :, 2 * B :].astype(F32)
        fin[l, 0:1, 0 : 2 * B] = jnp.sum(low * low, 0, keepdims=True)
        fin[l, 0:1, 2 * B :] = jnp.sum(high * high, 0, keepdims=True)

    @pl.loop(0, mine)
    def _(l):
        arrived(ublk.at[l, 1 - odd], recv_u.at[l])
        for whose, blocks in enumerate((EVEN, ODD)):
            for k, (rb, cb) in enumerate(blocks):
                factor[rb * B : (rb + 1) * B, cb * B : (cb + 1) * B] = ublk[l, whose, k]
        u1 = factor[:, 0 : 2 * B]
        u21 = factor[2 * B :, 0 : 2 * B]
        u2 = factor[2 * B :, 2 * B :]
        cov[0 : 2 * B, 0 : 2 * B] = transposed_dot(u1, u1).astype(BF16)
        cov[0 : 2 * B, 2 * B :] = transposed_dot(u21, u2).astype(BF16)
        cov[2 * B :, 0 : 2 * B] = transposed_dot(u2, u21).astype(BF16)
        cov[2 * B :, 2 * B :] = transposed_dot(u2, u2).astype(BF16)
        total = jnp.zeros((1, W), F32)
        for rb in range(4):
            rows = slice(rb * B, (rb + 1) * B)
            cross = -jnp.dot(cov[rows], mixed_half[l], preferred_element_type=F32)
            crossed[l, rows] = cross
            half = cross.astype(BF16).astype(F32)
            total = total + jnp.sum(half * mixed[l, rows], 0, keepdims=True)
        value = fld[pl.ds(base + l, 1)]
        fin[l, 0:1] = 0.5 * (fin[l, 0:1] - total - value * value)

    for most in range(2):
        @pl.when(mine == 3 + most)
        def _(most=most):
            arrived(coup.at[0 : 11 - most], send_c)
            for at in range(X):
                @pl.when(x == at)
                def _(at=at):
                    arrived(linv.at[0 : 11 - most, :, 0 : (at + 1) * B], send_l)

    @pl.loop(0, mine)
    def _(l):
        arrived(sbuf.at[l], recv_s.at[l])
        value = fld[pl.ds(base + l, 1)].astype(BF16)
        fin[l, 2:3] = lax.dot_general(value, sbuf[l], (((1,), (1,)), ((), ())), preferred_element_type=F32)
        for rb in range(4):
            rows = slice(rb * B, (rb + 1) * B)
            prod = sbuf[l, rows].astype(F32) * crossed[l, rows]
            prod = prod[:, 0:B] + prod[:, B : 2 * B] + prod[:, 2 * B : 3 * B] + prod[:, 3 * B :]
            fin[l, 1:2, rows] = jnp.sum(prod.T, 0, keepdims=True)

    for d in (2, 1, 3):
        remote(fin.at[:, :, at_block(plane(d))], got_x.at[x], send_f, recv_f, (leaf, plane(d))).start()
    got_x[x] = fin[:, :, at_block(x)]
    for most in range(2):
        @pl.when(mine == 3 + most)
        def _(most=most):
            arrived(sens.at[0 : 11 - most], send_s)

            @pl.when(x < 2)
            def _():
                arrived(picked.at[:, 0 : 4 - most, 0:4], send_u)

            @pl.when(x >= 2)
            def _():
                arrived(picked.at[:, 0 : 4 - most, 4:5], send_u)
    arrived(got_x.at[0 : X - 1], recv_f)

    sums = [jnp.zeros((GROUPS, B), F32), jnp.zeros((GROUPS, B), F32)]
    for xx in range(X):
        for l in range(MAXN):
            mask = masks[xx * MAXN + l]
            for q in range(2):
                sums[q] = sums[q] + mask * got_x[xx, l, q + 1 : q + 2]
    for p in range(GROUPS):
        for q in range(2):
            acc[p, q : q + 1] = sums[q][p : p + 1]

    @pl.loop(1, GROUPS)
    def _(d):
        to = (leaf + d) % GROUPS
        remote(acc.at[to], got_all.at[leaf], send_g, recv_g, (to, x)).start()

    got_all[leaf] = acc[leaf]
    arrived(got_x.at[0 : X - 1], send_f)
    for xx in range(X):
        for l in range(MAXN):
            def put(xx=xx, l=l):
                lg_out[pl.ds(first(xx) + l, 1)] = got_x[xx, l, 0:1]

            if l < MAXN - 1:
                put()
            else:
                pl.when(count(xx) == MAXN)(put)
    arrived(got_all.at[0 : GROUPS - 1], recv_g)
    last = jnp.sum(got_all[...], 0)
    cg_out[...] = last[0:1] - pfield[...].astype(F32) * last[1:2]
    arrived(got_all.at[0 : GROUPS - 1], send_g)


def body(parent_inverse, leaf_inverse, coupling, sensitivity, parent_of, leaf_field, parent_field):
    dma = pltpu.SemaphoreType.DMA
    hbm = pl.BlockSpec(memory_space=pltpu.HBM)
    vmem = pl.BlockSpec(memory_space=pltpu.VMEM)
    return pl.pallas_call(
        kernel,
        name="field_gradient",
        out_shape=(jax.ShapeDtypeStruct((14, B), F32), jax.ShapeDtypeStruct((1, B), F32)),
        in_specs=[pl.BlockSpec(memory_space=pltpu.SMEM), hbm, hbm, hbm, hbm, vmem, vmem],
        out_specs=(vmem, vmem),
        scratch_shapes=[
            pltpu.VMEM((MAXN, W, W), BF16),
            pltpu.VMEM((MAXN, W, W), BF16),
            pltpu.VMEM((MAXN, W, W), BF16),
            pltpu.VMEM((MAXN, 2, 5, B, B), BF16),
            pltpu.VMEM((MAXN, W, W), F32),
            pltpu.VMEM((MAXN, W, W), BF16),
            pltpu.VMEM((MAXN, W, W), F32),
            pltpu.VMEM((W, W), BF16),
            pltpu.VMEM((W, W), BF16),
            pltpu.VMEM((GROUPS, YFIRST, B, B), BF16),
            pltpu.VMEM((GROUPS, 5 - YFIRST, B, B), BF16),
            pltpu.VMEM((2, MAXN, 5, B, B), BF16),
            pltpu.VMEM((16, W), F32),
            pltpu.VMEM((X * MAXN, GROUPS, B), F32),
            pltpu.VMEM((MAXN, 4, W), F32),
            pltpu.VMEM((X, MAXN, 4, B), F32),
            pltpu.VMEM((GROUPS, 2, B), F32),
            pltpu.VMEM((GROUPS, 2, B), F32),
            dma, dma, dma, dma, dma, dma((2,)), dma((2,)), dma, dma,
            dma, dma((MAXN,)), dma((MAXN,)), dma((MAXN,)), dma((14,)), dma((14,)), dma((2,)), dma, dma,
        ],
        compiler_params=pltpu.CompilerParams(
            collective_id=0, has_side_effects=True, vmem_limit_bytes=64 * 2**20
        ),
    )(parent_of.reshape(1, 14), parent_inverse, leaf_inverse, coupling, sensitivity, leaf_field, parent_field)


def solution(mesh):
    in_specs = (
        P("leaf", None, "blk"),
        P("leaf", "blk", None),
        P("leaf", "blk", None),
        P("leaf", "blk", None),
        P("leaf", None),
        P("leaf", None),
        P("leaf", "blk"),
    )
    out_specs = (P("leaf", "blk"), P("leaf", "blk"))
    return jax.shard_map(body, mesh=mesh, in_specs=in_specs, out_specs=out_specs, check_vma=False)
```

time: 596 us -> 91.7 us (0.15)
  blocking collectives: 297 us -> 0 us
  waiting for transfers between devices: 241 us -> 0 us
  Pallas kernels: 0 us -> 88.4 us
  matrix products: 22.4 us -> 0 us
  between operations: 13.9 us -> 0.64 us
  local copies, waits for them, and re-layouts: 13.4 us -> 2.43 us
  other arithmetic: 7.09 us -> 0 us
    unnamed x1 -> x0, blocking collectives: 242 us -> none
    all_gather x3 -> x0, waiting for transfers between devices: 219 us -> none  [the longest x1 81.6 us: body(): lax.all_gather(cov_rows, 'leaf', axis=0, tiled=True)]
    pallas_call x0 -> x1, Pallas kernels: none -> 88.4 us  [body(): pl.pallas_call(kernel, name='field_gradient', out_shape=(jax.ShapeDtypeSt...]
    all_gather x2 -> x0, blocking collectives: 55.1 us -> none  [the longest x1 41.6 us: body(): lax.all_gather(parent_field, 'leaf', axis=0, tiled=True)]
    dot_general x6 -> x0, matrix products: 22.4 us -> none  [the longest x1 7.35 us: body(): jnp.einsum('lik,lia->kla', panel, cross_half, preferred_element_type=jnp....]
    reduce_scatter x2 -> x0, waiting for transfers between devices: 21.2 us -> none  [the longest x1 21.2 us: body(): lax.psum_scatter(partial_diag, 'blk', scatter_dimension=1, tiled=True)]
  transfers between devices with their start and end apart: 5 -> 0, of which waited for: 4 -> 0; matrix products, arithmetic and copies ran while one was open for 3% -> 0% of each run, Pallas kernels for 0% -> 0%
where the time goes in v1:
time: 91.7 us; the launch traced here: 91.5 us
  Pallas kernels  88.4 us (96%)
  local copies, waits for them, and re-layouts  2.43 us (3%)
    pallas_call x1, Pallas kernels, body(): pl.pallas_call(kernel, name='field_gradient', out_shape=(jax.ShapeDtypeSt...  88.4 us
    unnamed x2, local copies, waits for them, and re-layouts  2.43 us

profile of v1, /device:TPU:1, one launch (start us, length us, event | category | flops | bytes accessed | tf_op | source)
XLA Modules:
  0.0 91.5 jit_solution(7701248873077848454)
XLA Ops:
  0.6 88.4 %field_gradient.1 = (f32[14,128]{1,0:T(8,128)}, f32[1,128]{1,0:T(1,128)}) custom-call(s32[1,14]{1,0:T(1,128)} %bitcast.1, bf16[1,512,128]{2,1,0:T(8,128)(2,1)} %pinv.1, bf16[14,128,512]{2,1,0:T(8,128)(2,1)} %linv.1, bf16[14,128,512]{2,1,0:T(8,128)(2,1)} %coup.1, bf16[14,128,512]{2,1,0:T(8,128)(2,1)} %sens.1, bf16[14,512]{1,0:T(8,128)(2,1)} %field.1, ...), custom_call_target="tpu_custom_call" | custom-call | tf_op jit(solution)/shard_map/field_gradient/pallas_call | solution.py:436
  89.1 1.3 %copy.11 = f32[14,128]{1,0:T(8,128)} copy(f32[14,128]{1,0:T(8,128)} %get-tuple-element.4) | data formatting | bytes 14336
  90.4 1.1 %copy.12 = f32[1,128]{1,0:T(1,128)} copy(f32[1,128]{1,0:T(1,128)} %get-tuple-element.5) | data formatting | bytes 1024

commit v2 on v1

--- a/solution.py
+++ b/solution.py
@@ -12,6 +12,7 @@
 W = 512
 X, Y, Z = 4, 4, 8
 GROUPS = 64
+PAIRS = 32
 MAXN = 4
 EVEN = ((0, 0), (1, 0), (2, 0), (3, 0), (2, 2))
 ODD = ((1, 1), (2, 1), (3, 1), (3, 3), (3, 2))
@@ -30,7 +31,8 @@
     pof, pinv, linv, coup, sens, field, pfield,
     lg_out, cg_out,
     cbuf, lbuf, sbuf, ublk, mixed, mixed_half, crossed, factor, cov, ga, gb, picked,
-    fld, masks, fin, got_x, acc, got_all,
+    vc, vl, vs, fld, fin, got_x, acc, got_all,
+    load,
     send_p, send_c, send_l, send_s, send_u, send_ring, send_cross, send_f, send_g,
     recv_p, recv_cl, recv_s, recv_u, recv_a, recv_b, recv_cross, recv_f, recv_g,
 ):
@@ -60,21 +62,35 @@
     def arrived(ref, sem):
         pltpu.make_async_copy(ref, ref, sem).wait()
 
+    loads = [pltpu.make_async_copy(a, b, load.at[n]) for n, (a, b) in enumerate(((coup, vc), (linv, vl), (sens, vs)))]
+    for copy in loads:
+        copy.start()
+
+    chip = leaf // 2
+    other = leaf + 1 - 2 * c
+
+    def chip_at(n):
+        return (chip + (n + 15) % 31 + 1) % PAIRS
+
     barrier = pltpu.get_barrier_semaphore()
-    for d in range(1, X):
+
+    @pl.loop(0, PAIRS - 1)
+    def _(n):
+        pl.semaphore_signal(barrier, inc=1, device_id=(chip_at(n) * 2 + c, x), device_id_type=MESH)
+
+    for d in (2, 1, 3):
         pl.semaphore_signal(barrier, inc=1, device_id=(leaf, plane(d)), device_id_type=MESH)
-
-    @pl.loop(1, GROUPS)
-    def _(d):
-        pl.semaphore_signal(barrier, inc=1, device_id=((leaf + d) % GROUPS, x), device_id_type=MESH)
+    for d in (2, 1, 3, 0):
+        pl.semaphore_signal(barrier, inc=1, device_id=(other, plane(d)), device_id_type=MESH)
 
     zero = jnp.zeros((MAXN, B, B), BF16)
     lbuf[:, 0:B, B : 2 * B] = zero
     lbuf[:, 2 * B : 3 * B, 3 * B : 4 * B] = zero
     factor[0:B, B : 2 * B] = zero[0]
     factor[2 * B : 3 * B, 3 * B : 4 * B] = zero[0]
-    fin[...] = jnp.zeros_like(fin)
-    pl.semaphore_wait(barrier, X - 1 + GROUPS - 1)
+    fin[:, 0:3] = jnp.zeros((MAXN, 3, W), F32)
+    fin[:, 3:4] = jnp.full((MAXN, 1, W), -1.0, F32)
+    pl.semaphore_wait(barrier, PAIRS - 1 + 2 * X - 1)
 
     def slot_a(yy, zz, core=c):
         return core * 32 + zz * 4 + yy
@@ -100,13 +116,13 @@
                     remote(pinv.at[0, 3 * B :], own_slot(4), send_p, recv_p, (leaf, plane(d))).start()
 
     def c_copy(d, l):
-        return remote(coup.at[firsts[d] + l], cbuf.at[l, at_block(x)], send_c, recv_cl.at[l], (leaf, plane(d)))
+        return remote(vc.at[firsts[d] + l], cbuf.at[l, at_block(x)], send_c, recv_cl.at[l], (leaf, plane(d)))
 
     def s_copy(d, l):
-        return remote(sens.at[firsts[d] + l], sbuf.at[l, at_block(x)], send_s, recv_s.at[l], (leaf, plane(d)))
+        return remote(vs.at[firsts[d] + l], sbuf.at[l, at_block(x)], send_s, recv_s.at[l], (leaf, plane(d)))
 
     def l_copy(d, l, cb):
-        return remote(linv.at[firsts[d] + l, :, at_block(cb)], lbuf.at[l, at_block(x), at_block(cb)],
+        return remote(vl.at[firsts[d] + l, :, at_block(cb)], lbuf.at[l, at_block(x), at_block(cb)],
                       send_l, recv_cl.at[l], (leaf, plane(d)))
 
     def for_leaf(l, d, fn):
@@ -120,6 +136,8 @@
             for d in (1, 3, 2):
                 for_leaf(l, d, lambda l=l, d=d: s_copy(d, l).start())
 
+    loads[0].wait()
+    loads[1].wait()
     for l in range(MAXN):
         for d in (1, 3, 2):
             def send(l=l, d=d):
@@ -130,17 +148,18 @@
                     l_copy(d, l, cb).start()
 
             for_leaf(l, d, send)
+    loads[2].wait()
     send_s_panels(range(2))
 
     @pl.loop(0, mine)
     def _(l):
-        pltpu.make_async_copy(coup.at[base + l], cbuf.at[l, at_block(x)], recv_cl.at[l]).start()
-        pltpu.make_async_copy(sens.at[base + l], sbuf.at[l, at_block(x)], recv_s.at[l]).start()
+        pltpu.make_async_copy(vc.at[base + l], cbuf.at[l, at_block(x)], recv_cl.at[l]).start()
+        pltpu.make_async_copy(vs.at[base + l], sbuf.at[l, at_block(x)], recv_s.at[l]).start()
 
         @pl.loop(0, x + 1)
         def _(cb):
             pltpu.make_async_copy(
-                linv.at[base + l, :, at_block(cb)], lbuf.at[l, at_block(x), at_block(cb)], recv_cl.at[l]).start()
+                vl.at[base + l, :, at_block(cb)], lbuf.at[l, at_block(x), at_block(cb)], recv_cl.at[l]).start()
 
     def up(n, v, by):
         return (v + by) % n
@@ -305,13 +324,10 @@
         for_leaf(l, 0, keep)
 
     fld[0:14] = field[...].astype(F32)
-    place = lax.broadcasted_iota(jnp.int32, (GROUPS, B), 0)
-    for xx in range(X):
-        for l in range(MAXN):
-            p = pof[0, jnp.minimum(first(xx) + l, 13)]
-            if l == MAXN - 1:
-                p = jnp.where(count(xx) == MAXN, p, -1)
-            masks[xx * MAXN + l] = jnp.where(place == p, 1.0, 0.0)
+
+    @pl.loop(0, mine)
+    def _(l):
+        fin[l, 3:4] = jnp.full((1, W), pof[0, base + l].astype(F32))
 
     for at, blocks in enumerate((4, 3, 3, 1)):
         @pl.when(x == at)
@@ -363,11 +379,11 @@
     for most in range(2):
         @pl.when(mine == 3 + most)
         def _(most=most):
-            arrived(coup.at[0 : 11 - most], send_c)
+            arrived(vc.at[0 : 11 - most], send_c)
             for at in range(X):
                 @pl.when(x == at)
                 def _(at=at):
-                    arrived(linv.at[0 : 11 - most, :, 0 : (at + 1) * B], send_l)
+                    arrived(vl.at[0 : 11 - most, :, 0 : (at + 1) * B], send_l)
 
     @pl.loop(0, mine)
     def _(l):
@@ -380,13 +396,14 @@
             prod = prod[:, 0:B] + prod[:, B : 2 * B] + prod[:, 2 * B : 3 * B] + prod[:, 3 * B :]
             fin[l, 1:2, rows] = jnp.sum(prod.T, 0, keepdims=True)
 
-    for d in (2, 1, 3):
-        remote(fin.at[:, :, at_block(plane(d))], got_x.at[x], send_f, recv_f, (leaf, plane(d))).start()
-    got_x[x] = fin[:, :, at_block(x)]
+    for d in (2, 1, 3, 0):
+        for to in (other, leaf) if d else (other,):
+            remote(fin.at[:, :, at_block(plane(d))], got_x.at[c * X + x], send_f, recv_f, (to, plane(d))).start()
+    got_x[c * X + x] = fin[:, :, at_block(x)]
     for most in range(2):
         @pl.when(mine == 3 + most)
         def _(most=most):
-            arrived(sens.at[0 : 11 - most], send_s)
+            arrived(vs.at[0 : 11 - most], send_s)
 
             @pl.when(x < 2)
             def _():
@@ -395,38 +412,42 @@
             @pl.when(x >= 2)
             def _():
                 arrived(picked.at[:, 0 : 4 - most, 4:5], send_u)
-    arrived(got_x.at[0 : X - 1], recv_f)
-
-    sums = [jnp.zeros((GROUPS, B), F32), jnp.zeros((GROUPS, B), F32)]
-    for xx in range(X):
-        for l in range(MAXN):
-            mask = masks[xx * MAXN + l]
-            for q in range(2):
-                sums[q] = sums[q] + mask * got_x[xx, l, q + 1 : q + 2]
-    for p in range(GROUPS):
+    seven = got_x.at[0 : 2 * X - 1]
+    arrived(seven, recv_f)
+
+    place = (lax.broadcasted_iota(jnp.int32, (PAIRS, B), 0) * 2 + c).astype(F32)
+    sums = [jnp.zeros((PAIRS, B), F32), jnp.zeros((PAIRS, B), F32)]
+    for cc in range(2):
+        for xx in range(X):
+            for l in range(MAXN):
+                rows = got_x[cc * X + xx, l]
+                child = place == rows[3:4]
+                for q in range(2):
+                    sums[q] = sums[q] + jnp.where(child, rows[q + 1 : q + 2], 0.0)
+    for p in range(PAIRS):
         for q in range(2):
             acc[p, q : q + 1] = sums[q][p : p + 1]
 
-    @pl.loop(1, GROUPS)
-    def _(d):
-        to = (leaf + d) % GROUPS
-        remote(acc.at[to], got_all.at[leaf], send_g, recv_g, (to, x)).start()
-
-    got_all[leaf] = acc[leaf]
-    arrived(got_x.at[0 : X - 1], send_f)
+    @pl.loop(0, PAIRS - 1)
+    def _(n):
+        to = chip_at(n)
+        remote(acc.at[to], got_all.at[chip], send_g, recv_g, (to * 2 + c, x)).start()
+
+    got_all[chip] = acc[chip]
+    arrived(seven, send_f)
     for xx in range(X):
         for l in range(MAXN):
             def put(xx=xx, l=l):
-                lg_out[pl.ds(first(xx) + l, 1)] = got_x[xx, l, 0:1]
+                lg_out[pl.ds(first(xx) + l, 1)] = got_x[c * X + xx, l, 0:1]
 
             if l < MAXN - 1:
                 put()
             else:
                 pl.when(count(xx) == MAXN)(put)
-    arrived(got_all.at[0 : GROUPS - 1], recv_g)
+    arrived(got_all.at[0 : PAIRS - 1], recv_g)
     last = jnp.sum(got_all[...], 0)
     cg_out[...] = last[0:1] - pfield[...].astype(F32) * last[1:2]
-    arrived(got_all.at[0 : GROUPS - 1], send_g)
+    arrived(got_all.at[0 : PAIRS - 1], send_g)
 
 
 def body(parent_inverse, leaf_inverse, coupling, sensitivity, parent_of, leaf_field, parent_field):
@@ -452,12 +473,15 @@
             pltpu.VMEM((GROUPS, YFIRST, B, B), BF16),
             pltpu.VMEM((GROUPS, 5 - YFIRST, B, B), BF16),
             pltpu.VMEM((2, MAXN, 5, B, B), BF16),
+            pltpu.VMEM((14, B, W), BF16),
+            pltpu.VMEM((14, B, W), BF16),
+            pltpu.VMEM((14, B, W), BF16),
             pltpu.VMEM((16, W), F32),
-            pltpu.VMEM((X * MAXN, GROUPS, B), F32),
             pltpu.VMEM((MAXN, 4, W), F32),
-            pltpu.VMEM((X, MAXN, 4, B), F32),
-            pltpu.VMEM((GROUPS, 2, B), F32),
-            pltpu.VMEM((GROUPS, 2, B), F32),
+            pltpu.VMEM((2 * X, MAXN, 4, B), F32),
+            pltpu.VMEM((PAIRS, 2, B), F32),
+            pltpu.VMEM((PAIRS, 2, B), F32),
+            dma((3,)),
             dma, dma, dma, dma, dma, dma((2,)), dma((2,)), dma, dma,
             dma, dma((MAXN,)), dma((MAXN,)), dma((MAXN,)), dma((14,)), dma((14,)), dma((2,)), dma, dma,
         ],

time: 91.7 us -> 90 us (0.981)
  Pallas kernels: 88.4 us -> 86.8 us
    pallas_call x1, Pallas kernels: 88.4 us -> 86.8 us  [body(): pl.pallas_call(kernel, name='field_gradient', out_shape=(jax.ShapeDtypeSt...]
where the time goes in v2:
time: 90 us; the launch traced here: 89.8 us
  Pallas kernels  86.8 us (96%)
  local copies, waits for them, and re-layouts  2.43 us (3%)
    pallas_call x1, Pallas kernels, body(): pl.pallas_call(kernel, name='field_gradient', out_shape=(jax.ShapeDtypeSt...  86.8 us
    unnamed x2, local copies, waits for them, and re-layouts  2.43 us

profile of v2, /device:TPU:1, one launch (start us, length us, event | category | flops | bytes accessed | tf_op | source)
XLA Modules:
  0.0 89.8 jit_solution(16801079423741712629)
XLA Ops:
  0.6 86.8 %field_gradient.1 = (f32[14,128]{1,0:T(8,128)}, f32[1,128]{1,0:T(1,128)}) custom-call(s32[1,14]{1,0:T(1,128)} %bitcast.1, bf16[1,512,128]{2,1,0:T(8,128)(2,1)} %pinv.1, bf16[14,128,512]{2,1,0:T(8,128)(2,1)} %linv.1, bf16[14,128,512]{2,1,0:T(8,128)(2,1)} %coup.1, bf16[14,128,512]{2,1,0:T(8,128)(2,1)} %sens.1, bf16[14,512]{1,0:T(8,128)(2,1)} %field.1, ...), custom_call_target="tpu_custom_call" | custom-call | tf_op jit(solution)/shard_map/field_gradient/pallas_call | solution.py:457
  87.4 1.3 %copy.11 = f32[14,128]{1,0:T(8,128)} copy(f32[14,128]{1,0:T(8,128)} %get-tuple-element.4) | data formatting | bytes 14336
  88.7 1.1 %copy.12 = f32[1,128]{1,0:T(1,128)} copy(f32[1,128]{1,0:T(1,128)} %get-tuple-element.5) | data formatting | bytes 1024

commit v3 on v2

--- a/solution.py
+++ b/solution.py
@@ -29,7 +29,7 @@
 
 def kernel(
     pof, pinv, linv, coup, sens, field, pfield,
-    lg_out, cg_out,
+    out,
     cbuf, lbuf, sbuf, ublk, mixed, mixed_half, crossed, factor, cov, ga, gb, picked,
     vc, vl, vs, fld, fin, got_x, acc, got_all,
     load,
@@ -74,14 +74,16 @@
 
     barrier = pltpu.get_barrier_semaphore()
 
-    @pl.loop(0, PAIRS - 1)
-    def _(n):
-        pl.semaphore_signal(barrier, inc=1, device_id=(chip_at(n) * 2 + c, x), device_id_type=MESH)
+    def greet(*to):
+        pl.semaphore_signal(barrier, inc=1, device_id=to, device_id_type=MESH)
 
     for d in (2, 1, 3):
-        pl.semaphore_signal(barrier, inc=1, device_id=(leaf, plane(d)), device_id_type=MESH)
+        greet(leaf, plane(d))
     for d in (2, 1, 3, 0):
-        pl.semaphore_signal(barrier, inc=1, device_id=(other, plane(d)), device_id_type=MESH)
+        greet(other, plane(d))
+    for by in (1, -1):
+        greet((z + by) % Z * 8 + y * 2 + c, x)
+        greet(z * 8 + (y + by) % Y * 2 + c, x)
 
     zero = jnp.zeros((MAXN, B, B), BF16)
     lbuf[:, 0:B, B : 2 * B] = zero
@@ -90,7 +92,7 @@
     factor[2 * B : 3 * B, 3 * B : 4 * B] = zero[0]
     fin[:, 0:3] = jnp.zeros((MAXN, 3, W), F32)
     fin[:, 3:4] = jnp.full((MAXN, 1, W), -1.0, F32)
-    pl.semaphore_wait(barrier, PAIRS - 1 + 2 * X - 1)
+    pl.semaphore_wait(barrier, 2 * X - 1 + 4)
 
     def slot_a(yy, zz, core=c):
         return core * 32 + zz * 4 + yy
@@ -116,13 +118,13 @@
                     remote(pinv.at[0, 3 * B :], own_slot(4), send_p, recv_p, (leaf, plane(d))).start()
 
     def c_copy(d, l):
-        return remote(vc.at[firsts[d] + l], cbuf.at[l, at_block(x)], send_c, recv_cl.at[l], (leaf, plane(d)))
+        return remote((vc if l else coup).at[firsts[d] + l], cbuf.at[l, at_block(x)], send_c, recv_cl.at[l], (leaf, plane(d)))
 
     def s_copy(d, l):
         return remote(vs.at[firsts[d] + l], sbuf.at[l, at_block(x)], send_s, recv_s.at[l], (leaf, plane(d)))
 
     def l_copy(d, l, cb):
-        return remote(vl.at[firsts[d] + l, :, at_block(cb)], lbuf.at[l, at_block(x), at_block(cb)],
+        return remote((vl if l else linv).at[firsts[d] + l, :, at_block(cb)], lbuf.at[l, at_block(x), at_block(cb)],
                       send_l, recv_cl.at[l], (leaf, plane(d)))
 
     def for_leaf(l, d, fn):
@@ -136,9 +138,10 @@
             for d in (1, 3, 2):
                 for_leaf(l, d, lambda l=l, d=d: s_copy(d, l).start())
 
-    loads[0].wait()
-    loads[1].wait()
     for l in range(MAXN):
+        if l == 1:
+            loads[0].wait()
+            loads[1].wait()
         for d in (1, 3, 2):
             def send(l=l, d=d):
                 c_copy(d, l).start()
@@ -438,7 +441,7 @@
     for xx in range(X):
         for l in range(MAXN):
             def put(xx=xx, l=l):
-                lg_out[pl.ds(first(xx) + l, 1)] = got_x[c * X + xx, l, 0:1]
+                out[pl.ds(first(xx) + l, 1)] = got_x[c * X + xx, l, 0:1]
 
             if l < MAXN - 1:
                 put()
@@ -446,20 +449,25 @@
                 pl.when(count(xx) == MAXN)(put)
     arrived(got_all.at[0 : PAIRS - 1], recv_g)
     last = jnp.sum(got_all[...], 0)
-    cg_out[...] = last[0:1] - pfield[...].astype(F32) * last[1:2]
+    out[14:15] = last[0:1] - pfield[...].astype(F32) * last[1:2]
     arrived(got_all.at[0 : PAIRS - 1], send_g)
+
+
+def split_rows(rows, leaf_grad, coupling_grad):
+    leaf_grad[...] = rows[0:14]
+    coupling_grad[...] = rows[14:15]
 
 
 def body(parent_inverse, leaf_inverse, coupling, sensitivity, parent_of, leaf_field, parent_field):
     dma = pltpu.SemaphoreType.DMA
     hbm = pl.BlockSpec(memory_space=pltpu.HBM)
     vmem = pl.BlockSpec(memory_space=pltpu.VMEM)
-    return pl.pallas_call(
+    rows = pl.pallas_call(
         kernel,
         name="field_gradient",
-        out_shape=(jax.ShapeDtypeStruct((14, B), F32), jax.ShapeDtypeStruct((1, B), F32)),
+        out_shape=jax.ShapeDtypeStruct((16, B), F32),
         in_specs=[pl.BlockSpec(memory_space=pltpu.SMEM), hbm, hbm, hbm, hbm, vmem, vmem],
-        out_specs=(vmem, vmem),
+        out_specs=vmem,
         scratch_shapes=[
             pltpu.VMEM((MAXN, W, W), BF16),
             pltpu.VMEM((MAXN, W, W), BF16),
@@ -489,6 +497,13 @@
             collective_id=0, has_side_effects=True, vmem_limit_bytes=64 * 2**20
         ),
     )(parent_of.reshape(1, 14), parent_inverse, leaf_inverse, coupling, sensitivity, leaf_field, parent_field)
+    return pl.pallas_call(
+        split_rows,
+        name="split_rows",
+        out_shape=(jax.ShapeDtypeStruct((14, B), F32), jax.ShapeDtypeStruct((1, B), F32)),
+        in_specs=[vmem],
+        out_specs=(vmem, vmem),
+    )(rows)
 
 
 def solution(mesh):

time: 90 us -> 87.6 us (0.973)
  local copies, waits for them, and re-layouts: 2.43 us -> 0 us
    unnamed x2 -> x0, local copies, waits for them, and re-layouts: 2.43 us -> none
    pallas_call x1 -> x2, Pallas kernels: 86.8 us -> 86.7 us  [the longest x1 85.4 us: body(): pl.pallas_call(kernel, name='field_gradient', out_shape=jax.ShapeDtypeStr...]
where the time goes in v3:
time: 87.6 us; the launch traced here: 87.4 us
  Pallas kernels  86.7 us (99%)
    pallas_call x1, Pallas kernels, body(): pl.pallas_call(kernel, name='field_gradient', out_shape=jax.ShapeDtypeStr...  85.4 us

profile of v3, /device:TPU:1, one launch (start us, length us, event | category | flops | bytes accessed | tf_op | source)
XLA Modules:
  0.0 87.4 jit_solution(2232578206422162952)
XLA Ops:
  0.6 85.4 %field_gradient.1.rows = f32[16,128]{1,0:T(8,128)} custom-call(s32[1,14]{1,0:T(1,128)} %bitcast.1, bf16[1,512,128]{2,1,0:T(8,128)(2,1)} %pinv.1, bf16[14,128,512]{2,1,0:T(8,128)(2,1)} %linv.1, bf16[14,128,512]{2,1,0:T(8,128)(2,1)} %coup.1, bf16[14,128,512]{2,1,0:T(8,128)(2,1)} %sens.1, bf16[14,512]{1,0:T(8,128)(2,1)} %field.1, bf16[1,128]{1,0:T(2,128)(2,1)} %pfield.1), custom_call_target="tpu_custom_call" | custom-call | tf_op jit(solution)/shard_map/field_gradient/pallas_call | solution.py:465
  86.1 1.3 %split_rows.1 = (f32[14,128]{1,0:T(8,128)}, f32[1,128]{1,0:T(1,128)}) custom-call(f32[16,128]{1,0:T(8,128)} %field_gradient.1.rows), custom_call_target="tpu_custom_call" | custom-call | tf_op jit(solution)/shard_map/split_rows/pallas_call | solution.py:500

commit v4 on v3

--- a/solution.py
+++ b/solution.py
@@ -17,6 +17,20 @@
 EVEN = ((0, 0), (1, 0), (2, 0), (3, 0), (2, 2))
 ODD = ((1, 1), (2, 1), (3, 1), (3, 3), (3, 2))
 YFIRST = 2
+
+BELOW = (1, 4, 5, 1)
+
+
+def shares():
+    table = {}
+    for d, n in enumerate(BELOW):
+        table[(d - 1) % X, 0] = (0, n) if n > 2 else (5 - n, 5)
+        table[(d + 1) % X, 1] = (n, 5) if n > 2 else (0, 5 - n)
+    return table
+
+
+SHARES = shares()
+EARLY = 2
 
 
 def transposed_dot(a, b):
@@ -152,7 +166,7 @@
 
             for_leaf(l, d, send)
     loads[2].wait()
-    send_s_panels(range(2))
+    send_s_panels(range(EARLY))
 
     @pl.loop(0, mine)
     def _(l):
@@ -285,10 +299,9 @@
 
     odd = x % 2
 
-    def u_copy(i, l, some):
-        ref = picked.at[i, l, pl.ds(0, 4)] if some == 0 else picked.at[i, l, pl.ds(4, 1)]
-        dst = ublk.at[l, odd, pl.ds(0, 4)] if some == 0 else ublk.at[l, odd, pl.ds(4, 1)]
-        return remote(ref, dst, send_u, recv_u.at[l], (leaf, plane(1 + 2 * i)))
+    def u_copy(i, l, low, high):
+        return remote(picked.at[i, l, pl.ds(low, high - low)], ublk.at[l, odd, pl.ds(low, high - low)],
+                      send_u, recv_u.at[l], (leaf, plane(1 + 2 * i)))
 
     def chosen(j):
         p = pof[0, j]
@@ -304,19 +317,16 @@
             def pick(l=l, i=i):
                 block = chosen(firsts[1 + 2 * i] + l)
 
-                @pl.when(x < 2)
-                def _():
-                    for k in range(4):
-                        picked[i, l, k] = block[k]()
-                    u_copy(i, l, 0).start()
-
-                @pl.when(x >= 2)
-                def _():
-                    picked[i, l, 4] = block[4]()
-                    u_copy(i, l, 1).start()
+                for (at, way), (low, high) in SHARES.items():
+                    if way == i and high > low:
+                        @pl.when(x == at)
+                        def _(low=low, high=high):
+                            for k in range(low, high):
+                                picked[i, l, k] = block[k]()
+                            u_copy(i, l, low, high).start()
 
             for_leaf(l, 1 + 2 * i, pick)
-    send_s_panels(range(2, MAXN))
+    send_s_panels(range(EARLY, MAXN))
 
     for l in range(MAXN):
         def keep(l=l):
@@ -408,13 +418,11 @@
         def _(most=most):
             arrived(vs.at[0 : 11 - most], send_s)
 
-            @pl.when(x < 2)
-            def _():
-                arrived(picked.at[:, 0 : 4 - most, 0:4], send_u)
-
-            @pl.when(x >= 2)
-            def _():
-                arrived(picked.at[:, 0 : 4 - most, 4:5], send_u)
+            for (at, way), (low, high) in SHARES.items():
+                if high > low:
+                    @pl.when(x == at)
+                    def _(way=way, low=low, high=high):
+                        arrived(picked.at[way, 0 : 4 - most, low:high], send_u)
     seven = got_x.at[0 : 2 * X - 1]
     arrived(seven, recv_f)
 

time: 87.6 us -> 87.2 us (level)
  no operation moved by 1% of the time
where the time goes in v4:
time: 87.2 us; the launch traced here: 87 us
  Pallas kernels  86.4 us (99%)
    pallas_call x1, Pallas kernels, body(): pl.pallas_call(kernel, name='field_gradient', out_shape=jax.ShapeDtypeStr...  85.1 us

profile of v4, /device:TPU:1, one launch (start us, length us, event | category | flops | bytes accessed | tf_op | source)
XLA Modules:
  0.0 87.0 jit_solution(11452751695478110615)
XLA Ops:
  0.6 85.1 %field_gradient.1.rows = f32[16,128]{1,0:T(8,128)} custom-call(s32[1,14]{1,0:T(1,128)} %bitcast.1, bf16[1,512,128]{2,1,0:T(8,128)(2,1)} %pinv.1, bf16[14,128,512]{2,1,0:T(8,128)(2,1)} %linv.1, bf16[14,128,512]{2,1,0:T(8,128)(2,1)} %coup.1, bf16[14,128,512]{2,1,0:T(8,128)(2,1)} %sens.1, bf16[14,512]{1,0:T(8,128)(2,1)} %field.1, bf16[1,128]{1,0:T(2,128)(2,1)} %pfield.1), custom_call_target="tpu_custom_call" | custom-call | tf_op jit(solution)/shard_map/field_gradient/pallas_call | solution.py:473
  85.7 1.3 %split_rows.1 = (f32[14,128]{1,0:T(8,128)}, f32[1,128]{1,0:T(1,128)}) custom-call(f32[16,128]{1,0:T(8,128)} %field_gradient.1.rows), custom_call_target="tpu_custom_call" | custom-call | tf_op jit(solution)/shard_map/split_rows/pallas_call | solution.py:508

commit v5 on v4

--- a/solution.py
+++ b/solution.py
@@ -9,6 +9,7 @@
 F32 = jnp.float32
 BF16 = jnp.bfloat16
 B = 128
+H = 64
 W = 512
 X, Y, Z = 4, 4, 8
 GROUPS = 64
@@ -45,8 +46,8 @@
     pof, pinv, linv, coup, sens, field, pfield,
     out,
     cbuf, lbuf, sbuf, ublk, mixed, mixed_half, crossed, factor, cov, ga, gb, picked,
-    vc, vl, vs, fld, fin, got_x, acc, got_all,
-    load,
+    vc, vl, vs, packed, halves, fld, fin, got_x, acc, got_all,
+    load, send_d, recv_d,
     send_p, send_c, send_l, send_s, send_u, send_ring, send_cross, send_f, send_g,
     recv_p, recv_cl, recv_s, recv_u, recv_a, recv_b, recv_cross, recv_f, recv_g,
 ):
@@ -141,6 +142,26 @@
         return remote((vl if l else linv).at[firsts[d] + l, :, at_block(cb)], lbuf.at[l, at_block(x), at_block(cb)],
                       send_l, recv_cl.at[l], (leaf, plane(d)))
 
+    def l_half(d, l):
+        return remote((vl if l else linv).at[firsts[d] + l, H:B, at_block(x)],
+                      lbuf.at[l, pl.ds(pl.multiple_of(x * B + H, H), H), at_block(x)],
+                      send_l, recv_cl.at[l], (leaf, plane(d)))
+
+    low_lanes = lax.broadcasted_iota(jnp.int32, (H, B), 1) < H
+
+    def quarters(d, pair):
+        j = firsts[d] + 2 * pair
+        one = vl[j, 0:H, at_block(x)].astype(F32)
+        two = vl[jnp.minimum(j + 1, 13), 0:H, at_block(x)].astype(F32)
+        return jnp.where(low_lanes, one, pltpu.roll(two, H, 1)).astype(BF16)
+
+    def send_quarters():
+        for pair in range(2):
+            for d in (1, 3, 2):
+                packed[d, pair] = quarters(d, pair)
+                remote(packed.at[d, pair], halves.at[x, pair], send_d, recv_d, (leaf, plane(d))).start()
+            halves[x, pair] = quarters(0, pair)
+
     def for_leaf(l, d, fn):
         if l < MAXN - 1:
             fn()
@@ -156,13 +177,16 @@
         if l == 1:
             loads[0].wait()
             loads[1].wait()
+            send_quarters()
         for d in (1, 3, 2):
             def send(l=l, d=d):
                 c_copy(d, l).start()
 
-                @pl.loop(0, x + 1)
+                @pl.loop(0, x)
                 def _(cb):
                     l_copy(d, l, cb).start()
+
+                l_half(d, l).start()
 
             for_leaf(l, d, send)
     loads[2].wait()
@@ -173,7 +197,11 @@
         pltpu.make_async_copy(vc.at[base + l], cbuf.at[l, at_block(x)], recv_cl.at[l]).start()
         pltpu.make_async_copy(vs.at[base + l], sbuf.at[l, at_block(x)], recv_s.at[l]).start()
 
-        @pl.loop(0, x + 1)
+        pltpu.make_async_copy(
+            vl.at[base + l, H:B, at_block(x)],
+            lbuf.at[l, pl.ds(pl.multiple_of(x * B + H, H), H), at_block(x)], recv_cl.at[l]).start()
+
+        @pl.loop(0, x)
         def _(cb):
             pltpu.make_async_copy(
                 vl.at[base + l, :, at_block(cb)], lbuf.at[l, at_block(x), at_block(cb)], recv_cl.at[l]).start()
@@ -351,9 +379,17 @@
     arrived(ga.at[0:32], send_cross.at[0])
     arrived(gb.at[0:32], send_cross.at[1])
 
+    arrived(halves.at[0 : X - 1], recv_d)
+    for l in range(MAXN):
+        for rb in range(X):
+            quarter = halves[rb, l // 2].astype(F32)
+            if l % 2:
+                quarter = pltpu.roll(quarter, H, 1)
+            lbuf[l, rb * B : rb * B + H, rb * B : (rb + 1) * B] = jnp.where(low_lanes, quarter, 0.0).astype(BF16)
+
     @pl.loop(0, mine)
     def _(l):
-        arrived(ga.at[0:13], recv_cl.at[l])
+        arrived(ga.at[0:12], recv_cl.at[l])
 
         left = jnp.dot(cbuf[l], lbuf[l, :, 0 : 2 * B], preferred_element_type=F32)
         mixed[l, :, 0 : 2 * B] = left
@@ -389,6 +425,7 @@
         value = fld[pl.ds(base + l, 1)]
         fin[l, 0:1] = 0.5 * (fin[l, 0:1] - total - value * value)
 
+    arrived(packed.at[1:X], send_d)
     for most in range(2):
         @pl.when(mine == 3 + most)
         def _(most=most):
@@ -396,7 +433,9 @@
             for at in range(X):
                 @pl.when(x == at)
                 def _(at=at):
-                    arrived(vl.at[0 : 11 - most, :, 0 : (at + 1) * B], send_l)
+                    arrived(vl.at[0 : 11 - most, 0:H, 0:B], send_l)
+                    if at:
+                        arrived(vl.at[0 : 11 - most, :, 0 : at * B], send_l)
 
     @pl.loop(0, mine)
     def _(l):
@@ -492,12 +531,14 @@
             pltpu.VMEM((14, B, W), BF16),
             pltpu.VMEM((14, B, W), BF16),
             pltpu.VMEM((14, B, W), BF16),
+            pltpu.VMEM((X, 2, H, B), BF16),
+            pltpu.VMEM((X, 2, H, B), BF16),
             pltpu.VMEM((16, W), F32),
             pltpu.VMEM((MAXN, 4, W), F32),
             pltpu.VMEM((2 * X, MAXN, 4, B), F32),
             pltpu.VMEM((PAIRS, 2, B), F32),
             pltpu.VMEM((PAIRS, 2, B), F32),
-            dma((3,)),
+            dma((3,)), dma, dma,
             dma, dma, dma, dma, dma, dma((2,)), dma((2,)), dma, dma,
             dma, dma((MAXN,)), dma((MAXN,)), dma((MAXN,)), dma((14,)), dma((14,)), dma((2,)), dma, dma,
         ],

time: 87.2 us -> 86.2 us (0.989)
  Pallas kernels: 86.4 us -> 85.4 us
    pallas_call x1, Pallas kernels: 85.1 us -> 84.1 us  [body(): pl.pallas_call(kernel, name='field_gradient', out_shape=jax.ShapeDtypeStr...]
where the time goes in v5:
time: 86.2 us; the launch traced here: 86 us
  Pallas kernels  85.4 us (99%)
    pallas_call x1, Pallas kernels, body(): pl.pallas_call(kernel, name='field_gradient', out_shape=jax.ShapeDtypeStr...  84.1 us

profile of v5, /device:TPU:1, one launch (start us, length us, event | category | flops | bytes accessed | tf_op | source)
XLA Modules:
  0.0 86.0 jit_solution(17803086589224884363)
XLA Ops:
  0.6 84.1 %field_gradient.1.rows = f32[16,128]{1,0:T(8,128)} custom-call(s32[1,14]{1,0:T(1,128)} %bitcast.1, bf16[1,512,128]{2,1,0:T(8,128)(2,1)} %pinv.1, bf16[14,128,512]{2,1,0:T(8,128)(2,1)} %linv.1, bf16[14,128,512]{2,1,0:T(8,128)(2,1)} %coup.1, bf16[14,128,512]{2,1,0:T(8,128)(2,1)} %sens.1, bf16[14,512]{1,0:T(8,128)(2,1)} %field.1, bf16[1,128]{1,0:T(2,128)(2,1)} %pfield.1), custom_call_target="tpu_custom_call" | custom-call | tf_op jit(solution)/shard_map/field_gradient/pallas_call | solution.py:512
  84.7 1.3 %split_rows.1 = (f32[14,128]{1,0:T(8,128)}, f32[1,128]{1,0:T(1,128)}) custom-call(f32[16,128]{1,0:T(8,128)} %field_gradient.1.rows), custom_call_target="tpu_custom_call" | custom-call | tf_op jit(solution)/shard_map/split_rows/pallas_call | solution.py:549

commit v6 on v5

--- a/solution.py
+++ b/solution.py
@@ -43,11 +43,11 @@
 
 
 def kernel(
-    pof, pinv, linv, coup, sens, field, pfield,
+    parents, pinv, linv, coup, sens, fields, pfields,
     out,
     cbuf, lbuf, sbuf, ublk, mixed, mixed_half, crossed, factor, cov, ga, gb, picked,
     vc, vl, vs, packed, halves, fld, fin, got_x, acc, got_all,
-    load, send_d, recv_d,
+    pof, field, pfield, load, send_d, recv_d,
     send_p, send_c, send_l, send_s, send_u, send_ring, send_cross, send_f, send_g,
     recv_p, recv_cl, recv_s, recv_u, recv_a, recv_b, recv_cross, recv_f, recv_g,
 ):
@@ -77,7 +77,7 @@
     def arrived(ref, sem):
         pltpu.make_async_copy(ref, ref, sem).wait()
 
-    loads = [pltpu.make_async_copy(a, b, load.at[n]) for n, (a, b) in enumerate(((coup, vc), (linv, vl), (sens, vs)))]
+    loads = [pltpu.make_async_copy(a, b, load.at[n]) for n, (a, b) in enumerate(((coup, vc), (linv, vl), (sens, vs), (parents, pof), (fields, field), (pfields, pfield)))]
     for copy in loads:
         copy.start()
 
@@ -340,6 +340,7 @@
         b = half + yy * 8 + zz
         return [lambda k=k: ga[a, k] for k in range(YFIRST)] + [lambda k=k: gb[b, k] for k in range(5 - YFIRST)]
 
+    loads[3].wait()
     for l in range(MAXN):
         for i in range(2):
             def pick(l=l, i=i):
@@ -364,6 +365,8 @@
 
         for_leaf(l, 0, keep)
 
+    loads[4].wait()
+    loads[5].wait()
     fld[0:14] = field[...].astype(F32)
 
     @pl.loop(0, mine)
@@ -513,7 +516,7 @@
         kernel,
         name="field_gradient",
         out_shape=jax.ShapeDtypeStruct((16, B), F32),
-        in_specs=[pl.BlockSpec(memory_space=pltpu.SMEM), hbm, hbm, hbm, hbm, vmem, vmem],
+        in_specs=[hbm] * 7,
         out_specs=vmem,
         scratch_shapes=[
             pltpu.VMEM((MAXN, W, W), BF16),
@@ -538,7 +541,10 @@
             pltpu.VMEM((2 * X, MAXN, 4, B), F32),
             pltpu.VMEM((PAIRS, 2, B), F32),
             pltpu.VMEM((PAIRS, 2, B), F32),
-            dma((3,)), dma, dma,
+            pltpu.SMEM((1, 14), jnp.int32),
+            pltpu.VMEM((14, W), BF16),
+            pltpu.VMEM((1, B), BF16),
+            dma((6,)), dma, dma,
             dma, dma, dma, dma, dma, dma((2,)), dma((2,)), dma, dma,
             dma, dma((MAXN,)), dma((MAXN,)), dma((MAXN,)), dma((14,)), dma((14,)), dma((2,)), dma, dma,
         ],

time: 86.2 us -> 85.5 us (level)
  no operation moved by 1% of the time
where the time goes in v6:
time: 85.5 us; the launch traced here: 85.3 us
  Pallas kernels  84.7 us (99%)
    pallas_call x1, Pallas kernels, body(): pl.pallas_call(kernel, name='field_gradient', out_shape=jax.ShapeDtypeStr...  83.4 us

profile of v6, /device:TPU:1, one launch (start us, length us, event | category | flops | bytes accessed | tf_op | source)
XLA Modules:
  0.0 85.3 jit_solution(4548226091307578726)
XLA Ops:
  0.6 83.4 %field_gradient.1.rows = f32[16,128]{1,0:T(8,128)} custom-call(s32[1,14]{1,0:T(1,128)} %bitcast.1, bf16[1,512,128]{2,1,0:T(8,128)(2,1)} %pinv.1, bf16[14,128,512]{2,1,0:T(8,128)(2,1)} %linv.1, bf16[14,128,512]{2,1,0:T(8,128)(2,1)} %coup.1, bf16[14,128,512]{2,1,0:T(8,128)(2,1)} %sens.1, bf16[14,512]{1,0:T(8,128)(2,1)} %fields.1, bf16[1,128]{1,0:T(2,128)(2,1)} %pfields.1), custom_call_target="tpu_custom_call" | custom-call | tf_op jit(solution)/shard_map/field_gradient/pallas_call | solution.py:515
  84.0 1.3 %split_rows.1 = (f32[14,128]{1,0:T(8,128)}, f32[1,128]{1,0:T(1,128)}) custom-call(f32[16,128]{1,0:T(8,128)} %field_gradient.1.rows), custom_call_target="tpu_custom_call" | custom-call | tf_op jit(solution)/shard_map/split_rows/pallas_call | solution.py:555
